TPU v7x, 32 devices: a whole 2x2x4 slice. The times are simulated.
32 devices in a mesh: shift: 4 (over y, x), rows: 8 (over z, core).
Axes of the slice: x: 2, y: 2, z: 4, core: 2. Of those that a mesh axis runs over, the one named last changes fastest.
Arguments:
- zc_in: bfloat16 [4, 512, 16384], P('shift', 'rows'), may hold values from -6 to 6
- zo_in: bfloat16 [4, 384, 16384], P('shift', 'rows'), may hold values from -6 to 6
- count_c: int32 [4], replicated, may hold values from 256 to 512, as said below
- count_o: int32 [4], replicated, may hold values from 192 to 384, as said below
- mass: bfloat16 [128, 4, 128, 128], P(('shift', 'rows')), may hold values from -0.25 to 0.25
- adjacency: int32 [128, 4], P(('shift', 'rows')), may hold values from 0 to 127, as said below
- ghost_len: int32 [128, 4], P(('shift', 'rows')), may hold values from 1 to 128, as said below
- omega: float32 [2048, 128], replicated, may hold values from -6 to 6
Outputs:
- proj_c: float32 [128, 16384], P(None, ('shift', 'rows'))
- proj_o: float32 [128, 16384], P(None, ('shift', 'rows'))
Inputs may be any that keep to these rules, and one draw needn't show every extreme that they name: `count_c`: each entry is 256 or more, and one group holds 512 exactly. `count_o`: each entry is 192 or more, and one group holds 384 exactly. adjacency[i, 0] = i, and every entry lies within 2 blocks of i. ghost_len[i, 0] = 128.
All inputs are finite; a program needn't handle non-finite values.
Results may differ from a plain program's by a relative error of at most 0.0047.
Values may be sent and summed in bfloat16 or wider, within the bound.
A program may use at most 128 MiB of HBM per device.

v0:
```python
import jax
import jax.numpy as jnp
from jax import lax
from jax.sharding import PartitionSpec as P

REACH = 2
AXES = ("shift", "rows")
F32 = jnp.float32
BF16 = jnp.bfloat16


def split(matrix):
    high = lax.reduce_precision(matrix, 8, 7)
    return jnp.concatenate([high.astype(BF16), (matrix - high).astype(BF16)], axis=-1)


def joined(matrix):
    half = matrix.shape[-1] // 2
    return matrix[..., :half] + matrix[..., half:]


def dot(left, right, contract_left, contract_right):
    return lax.dot_general(
        left, right, (((contract_left,), (contract_right,)), ((), ())), preferred_element_type=F32
    )


def live(counts, slots):
    inner = jnp.arange(slots, dtype=jnp.int32)
    return (inner[None, :] < counts[:, None]).reshape(-1, 1)


def orth_local(matrix):
    square = jnp.dot(matrix.T, matrix, precision=lax.Precision.HIGHEST)
    lower = jnp.linalg.cholesky(square)
    return jax.scipy.linalg.solve_triangular(lower, matrix.T, lower=True).T


def per_device(zc_in, zo_in, count_c, count_o, mass, adjacency, ghost_len, omega):
    index = lax.axis_index(AXES)
    devices = lax.axis_size(AXES)
    zc = lax.all_to_all(zc_in[0], AXES, split_axis=1, concat_axis=0, tiled=True)
    zo = lax.all_to_all(zo_in[0], AXES, split_axis=1, concat_axis=0, tiled=True)
    groups = count_c.shape[0]
    live_c = live(count_c, zc.shape[0] // groups)
    live_o = live(count_o, zo.shape[0] // groups)
    size = mass.shape[2]
    count, near = adjacency.shape
    local = adjacency - index * count + REACH
    inner = jnp.arange(size, dtype=jnp.int32)
    masked = jnp.where(inner < ghost_len[:, :, None, None], mass, jnp.zeros_like(mass))
    places = jnp.arange(count + 2 * REACH, dtype=jnp.int32)
    hit = (local[:, :, None] == places)[:, :, None, :, None]
    dense = jnp.where(hit, masked[:, :, :, None, :].astype(F32), 0.0).sum(axis=1)
    dense = dense.reshape(count * size, -1)
    banded = lax.reduce_precision(dense, 8, 7)
    banded_rest = (dense - banded).astype(BF16)
    banded = banded.astype(BF16)
    up = [(i, i + 1) for i in range(devices - 1)]
    down = [(j, i) for i, j in up]
    edge = REACH * size
    width = omega.shape[1]

    def forward(right):
        rows = joined(dot(zc, split(right), 0, 0))
        before = lax.ppermute(rows[-edge:], AXES, up)
        after = lax.ppermute(rows[:edge], AXES, down)
        wide = split(jnp.concatenate([before, rows, after], axis=0))
        mixed = joined(dot(banded, wide, 1, 0) + dot(banded_rest, wide, 1, 0))
        part = joined(dot(zo, split(mixed), 1, 0))
        return jnp.where(live_o, lax.psum(part, AXES), 0.0)

    def backward(left):
        rows = dot(zo, split(left), 0, 0)
        rows = split(joined(rows))
        wide = joined(dot(banded, rows, 0, 0) + dot(banded_rest, rows, 0, 0))
        above = lax.ppermute(wide[-edge:], AXES, up)
        below = lax.ppermute(wide[:edge], AXES, down)
        rows = wide[edge:-edge]
        rows = rows + jnp.pad(above, ((0, rows.shape[0] - edge), (0, 0)))
        rows = rows + jnp.pad(below, ((rows.shape[0] - edge, 0), (0, 0)))
        part = joined(dot(zc, split(rows), 1, 0))
        return jnp.where(live_c, lax.psum(part, AXES), 0.0)

    first = orth_local(forward(jnp.where(live_c, omega, 0.0)))
    right = orth_local(backward(first))
    proj_c = dot(right.astype(BF16), zc, 0, 0)
    left = orth_local(forward(right))
    proj_o = dot(left.astype(BF16), zo, 0, 0)
    return (proj_c, proj_o)


def solution(mesh):
    placed = (
        P("shift", "rows", None),
        P("shift", "rows", None),
        P(),
        P(),
        P(AXES, None, None, None),
        P(AXES, None),
        P(AXES, None),
        P(),
    )
    return jax.shard_map(
        per_device,
        mesh=mesh,
        in_specs=placed,
        out_specs=(P(None, AXES), P(None, AXES)),
        check_vma=False,
    )
```

profile of v0, /device:TPU:0, one launch (start us, length us, event | category | flops | bytes accessed | tf_op | source)
XLA Modules:
  0.0 631.2 jit_solution(16880807980116318967)
XLA Ops:
  7.2 2.4 copy.38
  9.5 2.5 copy.31
  12.0 7.3 %all-to-all-start = ((bf16[64,32,512]{2,0,1:T(8,128)(2,1)}), bf16[64,32,512]{2,0,1:T(8,128)(2,1)S(1)}, u32[]{:S(2)}, u32[]{:S(2)}) async-start(bf16[64,32,512]{2,0,1:T(8,128)(2,1)} %copy.31), calls=%async_computation | async-start | bytes 4194304 | tf_op jit(solution)/shard_map/all_to_all | solution.py:42
  19.3 2.0 copy.39
  21.3 2.0 copy.32
  23.4 46.0 %all-to-all-done = bf16[64,32,512]{2,0,1:T(8,128)(2,1)S(1)} async-done(((bf16[64,32,512]{2,0,1:T(8,128)(2,1)}), bf16[64,32,512]{2,0,1:T(8,128)(2,1)S(1)}, u32[]{:S(2)}, u32[]{:S(2)}) %all-to-all-start) | async-done | bytes 2097184 | tf_op jit(solution)/shard_map/all_to_all | solution.py:42
  69.4 3.5 all-to-all-start.1
  73.1 1.6 copy.30
  74.7 1.1 select_convert_fusion
  76.0 0.7 convolution_bitcast_fusion.6
  76.8 2.0 collective-permute-start
  78.8 1.3 collective-permute-start.1
  80.1 0.9 select_reduce_fusion
  81.0 2.2 collective-permute-done.1
  84.4 27.3 %all-to-all-done.1 = bf16[48,32,512]{2,0,1:T(8,128)(2,1)} async-done(((bf16[48,32,512]{2,0,1:T(8,128)(2,1)}), bf16[48,32,512]{2,0,1:T(8,128)(2,1)}, u32[]{:S(2)}, u32[]{:S(2)}) %all-to-all-start.1) | async-done | bytes 1572896 | tf_op jit(solution)/shard_map/all_to_all | solution.py:43
  111.8 2.0 convolution_bitcast_fusion.1
  113.8 1.0 slice_add_fusion.2
  115.4 129.2 %all-reduce.6.cloned.1.call-done = f32[1536,128]{0,1:T(8,128)} async-done(((f32[1536,128]{0,1:T(8,128)}), f32[1536,128]{0,1:T(8,128)}) %all-reduce.6.cloned.1.call-update) | async-done | bytes 786448 | tf_op jit(solution)/shard_map/psum | solution.py:71
  244.6 2.2 fusion.23
  247.0 11.7 %cholesky.59 = f32[128,128]{1,0:T(8,128)S(1)} custom-call(f32[128,128]{1,0:T(8,128)S(1)} %fusion.66), custom_call_target="Cholesky" | custom-call | tf_op jit(solution)/shard_map/jit(cholesky)/cholesky | solution.py:35
  259.4 0.7 fusion.58
  260.0 9.8 %custom-call.11 = f32[1,128,128]{1,2,0:T(8,128)S(1)} custom-call(f32[1,128,128]{2,1,0:T(8,128)S(1)} %fusion.58), custom_call_target="InvertDiagBlocksLowerTriangular" | custom-call | tf_op jit(solution)/shard_map/jit(_solve_triangular)/triangular_solve | solution.py:36
  269.8 2.0 reduce-precision_convert_fusion.3
  271.8 2.0 convolution_bitcast_fusion.5
  275.0 1.4 collective-permute-start.2
  276.4 1.3 collective-permute-start.3
  277.8 3.6 collective-permute-done.3
  281.4 0.7 convolution_bitcast_fusion.2
  282.1 1.1 slice_add_fusion
  283.5 136.5 %all-reduce.8.cloned.1.call-done = f32[2048,128]{0,1:T(8,128)} async-done(((f32[2048,128]{0,1:T(8,128)}), f32[2048,128]{0,1:T(8,128)}) %all-reduce.8.cloned.1.call-update) | async-done | bytes 1048592 | tf_op jit(solution)/shard_map/psum | solution.py:83
  420.0 2.7 fusion.11
  422.8 11.7 %cholesky.70 = f32[128,128]{1,0:T(8,128)S(1)} custom-call(f32[128,128]{1,0:T(8,128)S(1)} %fusion.64), custom_call_target="Cholesky" | custom-call | tf_op jit(solution)/shard_map/jit(cholesky)/cholesky | solution.py:35
  435.8 9.8 %custom-call.9 = f32[1,128,128]{1,2,0:T(8,128)S(1)} custom-call(f32[1,128,128]{2,1,0:T(8,128)S(1)} %fusion.59), custom_call_target="InvertDiagBlocksLowerTriangular" | custom-call | tf_op jit(solution)/shard_map/jit(_solve_triangular)/triangular_solve | solution.py:36
  445.6 2.0 reduce-precision_convert_fusion.1
  447.6 0.7 convolution_bitcast_fusion.4
  448.4 1.3 collective-permute-start.4
  449.7 1.5 collective-permute-start.5
  451.2 3.4 collective-permute-done.5
  455.8 2.0 convolution_bitcast_fusion
  457.9 1.0 slice_add_fusion.1
  458.9 0.9 copy-done.3
  459.8 1.2 fusion.27
  461.0 133.8 %all-reduce.10.cloned.1.call-done = f32[1536,128]{0,1:T(8,128)} async-done(((f32[1536,128]{0,1:T(8,128)}), f32[1536,128]{0,1:T(8,128)}) %all-reduce.10.cloned.1.call-update) | async-done | bytes 786448 | tf_op jit(solution)/shard_map/psum | solution.py:71
  594.8 2.2 fusion.20
  597.1 11.7 %cholesky.81 = f32[128,128]{1,0:T(8,128)S(1)} custom-call(f32[128,128]{1,0:T(8,128)S(1)} %fusion.62), custom_call_target="Cholesky" | custom-call | tf_op jit(solution)/shard_map/jit(cholesky)/cholesky | solution.py:35
  610.2 9.8 %custom-call.12 = f32[1,128,128]{1,2,0:T(8,128)S(1)} custom-call(f32[1,128,128]{2,1,0:T(8,128)S(1)} %fusion.60), custom_call_target="InvertDiagBlocksLowerTriangular" | custom-call | tf_op jit(solution)/shard_map/jit(_solve_triangular)/triangular_solve | solution.py:36
  620.0 2.0 convolution_convert_fusion
  622.0 2.5 fusion.92
  (68 shorter events, 8.8 us)
Async XLA Ops:
  12.0 57.4 %all-to-all-start = ((bf16[64,32,512]{2,0,1:T(8,128)(2,1)}), bf16[64,32,512]{2,0,1:T(8,128)(2,1)S(1)}, u32[]{:S(2)}, u32[]{:S(2)}) async-start(bf16[64,32,512]{2,0,1:T(8,128)(2,1)} %copy.31), calls=%async_computation | async-start | bytes 4194304 | tf_op jit(solution)/shard_map/all_to_all | solution.py:42
  21.3 2.0 copy-start.6
  23.3 49.7 %copy-start.8 = (s32[4]{0:T(128)S(1)}, s32[4]{0:T(128)}, u32[]{:S(2)}) copy-start(s32[4]{0:T(128)} %param.13) | copy-start | bytes 52
  23.4 51.2 %copy-start.7 = (s32[4,4]{1,0:T(4,128)S(1)}, s32[4,4]{1,0:T(4,128)}, u32[]{:S(2)}) copy-start(s32[4,4]{1,0:T(4,128)} %param.17) | copy-start | bytes 196
  69.4 6.6 %copy-start = (bf16[64,32,512]{2,0,1:T(8,128)(2,1)}, bf16[64,32,512]{2,0,1:T(8,128)(2,1)S(1)}, u32[]{:S(2)}) copy-start(bf16[64,32,512]{2,0,1:T(8,128)(2,1)S(1)} %all-to-all-done) | copy-start | bytes 6291460
  69.4 42.4 %all-to-all-start.1 = ((bf16[48,32,512]{2,0,1:T(8,128)(2,1)}), bf16[48,32,512]{2,0,1:T(8,128)(2,1)}, u32[]{:S(2)}, u32[]{:S(2)}) async-start(bf16[48,32,512]{2,0,1:T(8,128)(2,1)} %copy.32), calls=%async_computation.1 | async-start | bytes 3145728 | tf_op jit(solution)/shard_map/all_to_all | solution.py:43
  72.9 171.7 %all-reduce.6.cloned.1.call-start = ((), (), s32[]{:S(2)}) async-start(), calls=%async_computation.2 | async-start | bytes 1572864 | tf_op jit(solution)/shard_map/psum | solution.py:71
  76.8 4.2 collective-permute-start
  78.8 4.4 collective-permute-start.1
  113.8 1.5 copy-start.9
  114.8 305.1 %all-reduce.8.cloned.1.call-start = ((), (), s32[]{:S(2)}) async-start(), calls=%async_computation.3 | async-start | bytes 2097152 | tf_op jit(solution)/shard_map/psum | solution.py:83
  274.9 6.5 %copy-start.1 = (bf16[64,32,512]{2,0,1:T(8,128)(2,1)S(1)}, bf16[64,32,512]{2,0,1:T(8,128)(2,1)}, u32[]{:S(2)}) copy-start(bf16[64,32,512]{2,0,1:T(8,128)(2,1)} %copy-done) | copy-start | bytes 6291460
  275.0 2.7 collective-permute-start.2
  276.4 4.9 collective-permute-start.3
  283.3 311.5 %all-reduce.10.cloned.1.call-start = ((), (), s32[]{:S(2)}) async-start(), calls=%async_computation.4 | async-start | bytes 1572864 | tf_op jit(solution)/shard_map/psum | solution.py:71
  419.9 25.7 %copy-start.4 = (f32[2048,128]{0,1:T(8,128)S(1)}, f32[2048,128]{0,1:T(8,128)}, u32[]{:S(2)}) copy-start(f32[2048,128]{0,1:T(8,128)} %all-reduce.8.cloned.1.call-done) | copy-start | bytes 3145732
  445.6 2.0 copy-start.2
  448.4 2.8 collective-permute-start.4
  449.7 4.9 collective-permute-start.5
  457.9 1.9 copy-start.3
  457.9 1.9 copy-start.5
Sparse Core Ops, SparseCore 0:
  114.9 129.6 all-reduce.5
  283.4 136.5 all-reduce.7
  459.0 135.7 all-reduce.9
where the time goes:
time: 638 us; the launch traced here: 631 us
  waiting for transfers between devices  482 us (76%)
  other arithmetic  74.7 us (12%)
  matrix products  27.9 us (4%)
  starting transfers between devices  20.3 us (3%)
  between operations  14.5 us (2%)
  local copies, waits for them, and re-layouts  11.7 us (2%)
    psum x2, waiting for transfers between devices, forward(): return jnp.where(live_o, lax.psum(part, AXES), 0.0)  263 us
    psum x1, waiting for transfers between devices, backward(): return jnp.where(live_c, lax.psum(part, AXES), 0.0)  136 us
    all_to_all x1, waiting for transfers between devices, per_device(): zc = lax.all_to_all(zc_in[0], AXES, split_axis=1, concat_axis=0, tiled=True)  46 us
    another operation x9, other arithmetic, orth_local(): lower = jnp.linalg.cholesky(square)  37.2 us
    another operation x6, other arithmetic, orth_local(): return jax.scipy.linalg.solve_triangular(lower, matrix.T, lower=True).T  31.4 us
    all_to_all x1, waiting for transfers between devices, per_device(): zo = lax.all_to_all(zo_in[0], AXES, split_axis=1, concat_axis=0, tiled=True)  27.3 us
    dot_general x14, matrix products, dot(): lax.dot_general(left, right, (((contract_left,), (contract_right,)), ((),...  14.9 us
  transfers between devices with their start and end apart: 11, of which 8 were waited for; matrix products, arithmetic and copies ran while one was open for 2% of the time, Pallas kernels for 0%

commit v1 on v0

--- a/solution.py
+++ b/solution.py
@@ -39,7 +39,10 @@
 def per_device(zc_in, zo_in, count_c, count_o, mass, adjacency, ghost_len, omega):
     index = lax.axis_index(AXES)
     devices = lax.axis_size(AXES)
-    zc = lax.all_to_all(zc_in[0], AXES, split_axis=1, concat_axis=0, tiled=True)
+    zc = jnp.concatenate(
+        lax.all_to_all(jnp.stack(jnp.split(zc_in[0], lax.axis_size(AXES), axis=1)), AXES, 0, 0),
+        axis=0,
+    )
     zo = lax.all_to_all(zo_in[0], AXES, split_axis=1, concat_axis=0, tiled=True)
     groups = count_c.shape[0]
     live_c = live(count_c, zc.shape[0] // groups)

time: 638 us -> 668 us (1.047)
  local copies, waits for them, and re-layouts: 11.7 us -> 38.9 us
    unnamed x24 -> x57, local copies, waits for them, and re-layouts: 6.85 us -> 35.9 us
  transfers between devices with their start and end apart: 11 -> 11, of which waited for: 8 -> 8; matrix products, arithmetic and copies ran while one was open for 2% -> 1% of each run, Pallas kernels for 0% -> 0%
where the time goes in v1:
time: 668 us; the launch traced here: 662 us
  waiting for transfers between devices  483 us (72%)
  other arithmetic  74.8 us (11%)
  local copies, waits for them, and re-layouts  38.9 us (6%)
  matrix products  29.6 us (4%)
  starting transfers between devices  20.3 us (3%)
  between operations  14.5 us (2%)
    psum x2, waiting for transfers between devices, forward(): return jnp.where(live_o, lax.psum(part, AXES), 0.0)  263 us
    psum x1, waiting for transfers between devices, backward(): return jnp.where(live_c, lax.psum(part, AXES), 0.0)  136 us
    all_to_all x1, waiting for transfers between devices, per_device(): lax.all_to_all(jnp.stack(jnp.split(zc_in[0], lax.axis_size(AXES), axis=1)...  46 us
    another operation x9, other arithmetic, orth_local(): lower = jnp.linalg.cholesky(square)  37.2 us
    unnamed x57, local copies, waits for them, and re-layouts  35.9 us
    another operation x6, other arithmetic, orth_local(): return jax.scipy.linalg.solve_triangular(lower, matrix.T, lower=True).T  31.4 us
    all_to_all x1, waiting for transfers between devices, per_device(): zo = lax.all_to_all(zo_in[0], AXES, split_axis=1, concat_axis=0, tiled=True)  28.8 us
    dot_general x14, matrix products, dot(): lax.dot_general(left, right, (((contract_left,), (contract_right,)), ((),...  15 us
  transfers between devices with their start and end apart: 11, of which 8 were waited for; matrix products, arithmetic and copies ran while one was open for 1% of the time, Pallas kernels for 0%

profile of v1, /device:TPU:0, one launch (start us, length us, event | category | flops | bytes accessed | tf_op | source)
XLA Modules:
  0.0 661.5 jit_solution(4786927188159072241)
XLA Ops:
  7.2 1.6 constant_dynamic-update-slice_fusion.31
  8.8 1.5 constant_dynamic-update-slice_fusion.30
  10.3 1.5 constant_dynamic-update-slice_fusion.29
  11.7 1.5 constant_dynamic-update-slice_fusion.28
  13.2 1.5 constant_dynamic-update-slice_fusion.27
  14.6 1.5 constant_dynamic-update-slice_fusion.26
  16.1 1.5 constant_dynamic-update-slice_fusion.25
  17.6 1.5 constant_dynamic-update-slice_fusion.24
  19.0 1.5 constant_dynamic-update-slice_fusion.23
  20.5 1.5 constant_dynamic-update-slice_fusion.22
  22.0 1.5 constant_dynamic-update-slice_fusion.21
  23.4 1.5 constant_dynamic-update-slice_fusion.20
  24.9 1.5 constant_dynamic-update-slice_fusion.19
  26.4 1.5 constant_dynamic-update-slice_fusion.18
  27.8 1.5 constant_dynamic-update-slice_fusion.17
  29.3 1.5 constant_dynamic-update-slice_fusion.16
  40.7 7.3 %all-to-all-start = ((bf16[32,64,512]{2,1,0:T(8,128)(2,1)}), bf16[32,64,512]{2,1,0:T(8,128)(2,1)S(1)}, u32[]{:S(2)}, u32[]{:S(2)}) async-start(bf16[32,64,512]{2,1,0:T(8,128)(2,1)} %constant_dynamic-update-slice_fusion), calls=%async_computation | async-start | bytes 4194304 | tf_op jit(solution)/shard_map/all_to_all | solution.py:43
  48.0 2.0 copy.30
  50.0 2.0 copy.24
  52.1 46.0 %all-to-all-done = bf16[32,64,512]{2,1,0:T(8,128)(2,1)S(1)} async-done(((bf16[32,64,512]{2,1,0:T(8,128)(2,1)}), bf16[32,64,512]{2,1,0:T(8,128)(2,1)S(1)}, u32[]{:S(2)}, u32[]{:S(2)}) %all-to-all-start) | async-done | bytes 2097184 | tf_op jit(solution)/shard_map/all_to_all | solution.py:43
  98.1 3.5 all-to-all-start.1
  104.2 2.0 collective-permute-start
  108.3 2.2 collective-permute-done.1
  111.7 28.8 %all-to-all-done.1 = bf16[48,32,512]{2,0,1:T(8,128)(2,1)} async-done(((bf16[48,32,512]{2,0,1:T(8,128)(2,1)}), bf16[48,32,512]{2,0,1:T(8,128)(2,1)}, u32[]{:S(2)}, u32[]{:S(2)}) %all-to-all-start.1) | async-done | bytes 1572896 | tf_op jit(solution)/shard_map/all_to_all | solution.py:46
  140.5 2.0 convolution_bitcast_fusion.1
  144.1 129.1 %all-reduce.6.cloned.1.call-done = f32[1536,128]{0,1:T(8,128)} async-done(((f32[1536,128]{0,1:T(8,128)}), f32[1536,128]{0,1:T(8,128)}) %all-reduce.6.cloned.1.call-update) | async-done | bytes 786448 | tf_op jit(solution)/shard_map/psum | solution.py:74
  273.3 2.2 fusion.25
  275.6 11.7 %cholesky.59 = f32[128,128]{1,0:T(8,128)S(1)} custom-call(f32[128,128]{1,0:T(8,128)S(1)} %fusion.69), custom_call_target="Cholesky" | custom-call | tf_op jit(solution)/shard_map/jit(cholesky)/cholesky | solution.py:35
  288.6 9.8 %custom-call.11 = f32[1,128,128]{1,2,0:T(8,128)S(1)} custom-call(f32[1,128,128]{2,1,0:T(8,128)S(1)} %fusion.61), custom_call_target="InvertDiagBlocksLowerTriangular" | custom-call | tf_op jit(solution)/shard_map/jit(_solve_triangular)/triangular_solve | solution.py:36
  298.4 2.0 reduce-precision_convert_fusion.3
  300.4 2.0 convolution_bitcast_fusion.3
  303.6 1.4 collective-permute-start.2
  306.4 3.6 collective-permute-done.3
  312.1 136.5 %all-reduce.8.cloned.1.call-done = f32[2048,128]{1,0:T(8,128)} async-done(((f32[2048,128]{1,0:T(8,128)}), f32[2048,128]{1,0:T(8,128)}) %all-reduce.8.cloned.1.call-update) | async-done | bytes 1048592 | tf_op jit(solution)/shard_map/psum | solution.py:86
  448.6 4.0 fusion.13
  452.7 11.7 %cholesky.70 = f32[128,128]{1,0:T(8,128)S(1)} custom-call(f32[128,128]{1,0:T(8,128)S(1)} %fusion.67), custom_call_target="Cholesky" | custom-call | tf_op jit(solution)/shard_map/jit(cholesky)/cholesky | solution.py:35
  465.8 9.8 %custom-call.9 = f32[1,128,128]{1,2,0:T(8,128)S(1)} custom-call(f32[1,128,128]{2,1,0:T(8,128)S(1)} %fusion.62), custom_call_target="InvertDiagBlocksLowerTriangular" | custom-call | tf_op jit(solution)/shard_map/jit(_solve_triangular)/triangular_solve | solution.py:36
  475.6 2.3 reduce-precision_convert_fusion.1
  478.7 1.3 collective-permute-start.4
  480.1 1.5 collective-permute-start.5
  481.6 3.4 collective-permute-done.5
  486.1 2.0 convolution_bitcast_fusion
  491.3 133.8 %all-reduce.10.cloned.1.call-done = f32[1536,128]{0,1:T(8,128)} async-done(((f32[1536,128]{0,1:T(8,128)}), f32[1536,128]{0,1:T(8,128)}) %all-reduce.10.cloned.1.call-update) | async-done | bytes 786448 | tf_op jit(solution)/shard_map/psum | solution.py:74
  625.1 2.2 fusion.22
  627.4 11.7 %cholesky.81 = f32[128,128]{1,0:T(8,128)S(1)} custom-call(f32[128,128]{1,0:T(8,128)S(1)} %fusion.65), custom_call_target="Cholesky" | custom-call | tf_op jit(solution)/shard_map/jit(cholesky)/cholesky | solution.py:35
  640.5 9.8 %custom-call.12 = f32[1,128,128]{1,2,0:T(8,128)S(1)} custom-call(f32[1,128,128]{2,1,0:T(8,128)S(1)} %fusion.63), custom_call_target="InvertDiagBlocksLowerTriangular" | custom-call | tf_op jit(solution)/shard_map/jit(_solve_triangular)/triangular_solve | solution.py:36
  650.3 2.0 convolution_convert_fusion
  652.3 2.5 fusion.95
  (101 shorter events, 31.4 us)
Async XLA Ops:
  7.2 23.6 %copy-start.5 = (bf16[1,64,16384]{2,1,0:T(8,128)(2,1)S(1)}, bf16[1,64,16384]{2,1,0:T(8,128)(2,1)}, u32[]{:S(2)}) copy-start(bf16[1,64,16384]{2,1,0:T(8,128)(2,1)} %param.11) | copy-start | bytes 6291460
  40.7 57.4 %all-to-all-start = ((bf16[32,64,512]{2,1,0:T(8,128)(2,1)}), bf16[32,64,512]{2,1,0:T(8,128)(2,1)S(1)}, u32[]{:S(2)}, u32[]{:S(2)}) async-start(bf16[32,64,512]{2,1,0:T(8,128)(2,1)} %constant_dynamic-update-slice_fusion), calls=%async_computation | async-start | bytes 4194304 | tf_op jit(solution)/shard_map/all_to_all | solution.py:43
  50.0 2.0 copy-start.8
  52.0 49.7 %copy-start.10 = (s32[4]{0:T(128)S(1)}, s32[4]{0:T(128)}, u32[]{:S(2)}) copy-start(s32[4]{0:T(128)} %param.13) | copy-start | bytes 52
  52.0 49.7 %copy-start.9 = (s32[4,4]{1,0:T(4,128)S(1)}, s32[4,4]{1,0:T(4,128)}, u32[]{:S(2)}) copy-start(s32[4,4]{1,0:T(4,128)} %param.17) | copy-start | bytes 196
  52.1 50.9 %copy-start.7 = (f32[2048,128]{1,0:T(8,128)S(1)}, f32[2048,128]{1,0:T(8,128)}, u32[]{:S(2)}) copy-start(f32[2048,128]{1,0:T(8,128)} %param.18) | copy-start | bytes 3145732
  98.1 5.2 copy-start
  98.1 42.3 %all-to-all-start.1 = ((bf16[48,32,512]{2,0,1:T(8,128)(2,1)}), bf16[48,32,512]{2,0,1:T(8,128)(2,1)}, u32[]{:S(2)}, u32[]{:S(2)}) async-start(bf16[48,32,512]{2,0,1:T(8,128)(2,1)} %copy.24), calls=%async_computation.1 | async-start | bytes 3145728 | tf_op jit(solution)/shard_map/all_to_all | solution.py:46
  101.6 171.6 %all-reduce.6.cloned.1.call-start = ((), (), s32[]{:S(2)}) async-start(), calls=%async_computation.2 | async-start | bytes 1572864 | tf_op jit(solution)/shard_map/psum | solution.py:74
  104.2 4.2 collective-permute-start
  106.1 4.4 collective-permute-start.1
  142.5 1.5 copy-start.11
  143.5 305.1 %all-reduce.8.cloned.1.call-start = ((), (), s32[]{:S(2)}) async-start(), calls=%async_computation.3 | async-start | bytes 2097152 | tf_op jit(solution)/shard_map/psum | solution.py:86
  303.5 6.5 copy-start.1
  303.6 2.7 collective-permute-start.2
  305.1 4.9 collective-permute-start.3
  311.9 313.2 %all-reduce.10.cloned.1.call-start = ((), (), s32[]{:S(2)}) async-start(), calls=%async_computation.4 | async-start | bytes 1572864 | tf_op jit(solution)/shard_map/psum | solution.py:74
  448.6 27.0 %copy-start.4 = (f32[2048,128]{1,0:T(8,128)S(1)}, f32[2048,128]{1,0:T(8,128)}, u32[]{:S(2)}) copy-start(f32[2048,128]{1,0:T(8,128)} %all-reduce.8.cloned.1.call-done) | copy-start | bytes 3145732
  475.6 2.3 copy-start.2
  478.7 2.8 collective-permute-start.4
  480.1 4.9 collective-permute-start.5
  488.2 1.9 copy-start.3
  488.2 1.9 copy-start.6
Sparse Core Ops, SparseCore 0:
  143.6 129.5 all-reduce.5
  312.0 136.5 all-reduce.7
  489.3 135.7 all-reduce.9
